TPU v7x, 32 devices: a whole 2x2x4 slice. The times are simulated.
32 devices in a mesh: ax: 16 (over z, y, x), rad: 2 (over core).
Axes of the slice: x: 2, y: 2, z: 4, core: 2. Of those that a mesh axis runs over, the one named last changes fastest.
Arguments:
- fields: float32 [128, 5, 8, 1024], P('ax', None, None, 'rad'), may hold values from -6 to 6
Outputs:
- axial_deriv: float32 [128, 5, 8, 1024], P('ax', None, None, 'rad')
- filtered: float32 [128, 5, 8, 1024], P('ax', None, None, 'rad')
- radial_deriv: float32 [128, 5, 8, 1024], P('ax', None, None, 'rad')
All inputs are finite; a program needn't handle non-finite values.
Results may differ from a plain program's by a relative error of at most 0.0003.
Values sent between devices are 32-bit elements; how exact they have to be, the bound alone decides.
A program may use at most 128 MiB of HBM per device.

v0:
```python
import jax
import jax.numpy as jnp
from jax import lax
from jax.sharding import PartitionSpec as P

deriv_alpha = 1.0 / 3.0
filter_alpha = 0.4999
block_rows = 64


def with_halo(array, sides, width):
    for axis, dim in sides:
        size, length = (lax.axis_size(axis), array.shape[dim])
        up = [(i, (i + 1) % size) for i in range(size - 1)]
        down = [(j, i) for i, j in up]
        last = lax.slice_in_dim(array, length - width, length, axis=dim)
        initial = lax.slice_in_dim(array, 0, width, axis=dim)
        before = lax.ppermute(last, axis, up)
        after = lax.ppermute(initial, axis, down)
        array = jnp.concatenate([before, array, after], axis=dim)
    return array


def filter_weights():
    return [
        (93.0 + 70.0 * filter_alpha) / 128.0,
        (7.0 + 18.0 * filter_alpha) / 16.0,
        (-7.0 + 14.0 * filter_alpha) / 32.0,
        (1.0 - 2.0 * filter_alpha) / 16.0,
        (-1.0 + 2.0 * filter_alpha) / 128.0,
    ]


def sources(padded, count):

    def shifted(k):
        return padded[4 + k : 4 + k + count]

    deriv_rhs = 7.0 / 9.0 * (shifted(1) - shifted(-1)) + 1.0 / 36.0 * (shifted(2) - shifted(-2))
    weights = filter_weights()
    filter_rhs = weights[0] * shifted(0)
    for n in range(1, 5):
        filter_rhs = filter_rhs + weights[n] / 2.0 * (shifted(n) + shifted(-n))
    return jnp.stack([deriv_rhs, filter_rhs])


def pivots(alpha, rows):
    root = (1.0 - 4.0 * alpha * alpha) ** 0.5
    big_root = (1.0 + root) / 2.0
    ratio = (1.0 - root) / (1.0 + root)
    return big_root * (1.0 - jnp.power(ratio, rows + 2.0)) / (1.0 - jnp.power(ratio, rows + 1.0))


def tables(alpha, rows):
    length = rows.shape[-1]
    piv = pivots(alpha, rows)
    before = pivots(alpha, jnp.maximum(rows - 1.0, 0.0))
    log_fwd = jnp.log(alpha / before)
    cum_fwd = jnp.cumsum(log_fwd, axis=-1)
    log_bwd = jnp.log(alpha / piv)
    cum_bwd = jnp.cumsum(log_bwd, axis=-1)
    excl_bwd = cum_bwd - log_bwd
    index = jnp.arange(length)
    parity = ((index[:, None] - index[None, :]) % 2).astype(jnp.float32)
    signs = 1.0 - 2.0 * parity
    lower = index[:, None] >= index[None, :]
    upper = index[:, None] <= index[None, :]
    diff_fwd = jnp.minimum(cum_fwd[..., :, None] - cum_fwd[..., None, :], 0.0)
    forward = jnp.where(lower, signs * jnp.exp(diff_fwd), 0.0)
    diff_bwd = jnp.minimum(excl_bwd[..., None, :] - excl_bwd[..., :, None], 0.0)
    backward = jnp.where(upper, signs * jnp.exp(diff_bwd) / piv[..., None, :], 0.0)
    sign_in = 1.0 - 2.0 * ((index + 1) % 2).astype(jnp.float32)
    gain_in = sign_in * jnp.exp(cum_fwd)
    sign_out = 1.0 - 2.0 * ((length - index) % 2).astype(jnp.float32)
    gain_out = sign_out * jnp.exp(cum_bwd[..., length - 1 :] - excl_bwd)
    return (forward, gain_in, backward, gain_out)


def combine(earlier, later):
    return (earlier[0] * later[0], later[1] + later[0] * earlier[1])


def solve(rhs, rows, chain_forward, chain_backward):
    parts = [tables(deriv_alpha, rows), tables(filter_alpha, rows)]
    forward = jnp.stack([parts[0][0], parts[1][0]])
    gain_in = jnp.stack([parts[0][1], parts[1][1]])
    backward = jnp.stack([parts[0][2], parts[1][2]])
    gain_out = jnp.stack([parts[0][3], parts[1][3]])
    local_fwd = jnp.einsum("sbkj,sbjl->sbkl", forward, rhs, precision=lax.Precision.HIGHEST)
    incoming = chain_forward(gain_in[:, :, -1:], local_fwd[:, :, -1, :])
    eliminated = local_fwd + gain_in[..., None] * incoming[:, :, None, :]
    local_bwd = jnp.einsum("sbkj,sbjl->sbkl", backward, eliminated, precision=lax.Precision.HIGHEST)
    outgoing = chain_backward(gain_out[:, :, :1], local_bwd[:, :, 0, :])
    return local_bwd + gain_out[..., None] * outgoing[:, :, None, :]


def block_chain(coeff, offset):
    inclusive = lax.associative_scan(combine, (coeff, offset), axis=1)
    return jnp.concatenate([jnp.zeros_like(offset[:, :1]), inclusive[1][:, :-1]], axis=1)


def block_forward(coeff, offset):
    return block_chain(coeff, offset)


def block_backward(coeff, offset):
    flipped = block_chain(jnp.flip(coeff, axis=1), jnp.flip(offset, axis=1))
    return jnp.flip(flipped, axis=1)


def body(fields):
    rows_dev, count, planes, radial = fields.shape
    width = count * planes * radial
    rimmed = with_halo(fields, (("rad", 3),), 3)

    def radial_cell(k):
        return rimmed[:, :, :, 3 + k : 3 + k + radial]

    radial_deriv = (
        45.0 * (radial_cell(1) - radial_cell(-1))
        - 9.0 * (radial_cell(2) - radial_cell(-2))
        + (radial_cell(3) - radial_cell(-3))
    ) / 60.0
    flat = fields.reshape(rows_dev, width)
    lines = lax.all_to_all(flat, "ax", split_axis=1, concat_axis=0, tiled=True)
    total = lines.shape[0]
    padded = jnp.pad(lines, ((4, 4), (0, 0)))
    rhs = sources(padded, total)
    blocks = total // block_rows
    rows = jnp.arange(total, dtype=jnp.float32).reshape(blocks, block_rows)
    solved = solve(rhs.reshape(2, blocks, block_rows, -1), rows, block_forward, block_backward)
    solved = solved.reshape(2, total, -1)
    result = lax.all_to_all(solved, "ax", split_axis=1, concat_axis=2, tiled=True)
    axial_deriv = result[0].reshape(fields.shape)
    filtered = result[1].reshape(fields.shape)
    return (axial_deriv, filtered, radial_deriv)


def solution(mesh):
    in_specs = (P("ax", None, None, "rad"),)
    out_specs = (P("ax", None, None, "rad"), P("ax", None, None, "rad"), P("ax", None, None, "rad"))
    return jax.shard_map(body, mesh=mesh, in_specs=in_specs, out_specs=out_specs, check_vma=False)
```

profile of v0, /device:TPU:8, one launch (start us, length us, event | category | flops | bytes accessed | tf_op | source)
XLA Modules:
  0.0 72.5 jit_solution(13071631974729192661)
XLA Ops:
  0.6 1.3 %all_to_all.25 = f32[8,16,1280]{2,1,0:T(8,128)S(1)} reshape(f32[8,5,8,512]{3,2,1,0:T(8,128)} %param.1) | data formatting | bytes 1310720 | tf_op jit(solution)/shard_map/all_to_all | solution.py:125
  1.9 1.2 %copy.11 = f32[8,16,1280]{2,0,1:T(8,128)} copy(f32[8,16,1280]{2,1,0:T(8,128)S(1)} %all_to_all.25) | data formatting | bytes 1310720 | tf_op jit(solution)/shard_map/all_to_all | solution.py:125
  3.2 7.2 %all-to-all-start = ((f32[8,16,1280]{2,0,1:T(8,128)}), f32[8,16,1280]{2,0,1:T(8,128)S(1)}, u32[]{:S(2)}, u32[]{:S(2)}) async-start(f32[8,16,1280]{2,0,1:T(8,128)} %copy.11), calls=%async_computation | async-start | bytes 1310720 | tf_op jit(solution)/shard_map/all_to_all | solution.py:125
  10.5 0.2 reduce_window_sum.36
  10.8 0.2 reduce_window_sum.29
  11.0 0.2 reduce_window_sum.28
  11.3 0.2 reduce_window_sum.27
  11.5 0.2 slice_reduce_fusion
  11.7 0.1 fusion.39
  11.8 0.1 fusion.49
  11.9 0.2 fusion.48
  12.2 0.1 divide_select_fusion.1
  12.4 15.2 %all-to-all-done = f32[8,16,1280]{2,0,1:T(8,128)S(1)} async-done(((f32[8,16,1280]{2,0,1:T(8,128)}), f32[8,16,1280]{2,0,1:T(8,128)S(1)}, u32[]{:S(2)}, u32[]{:S(2)}) %all-to-all-start) | async-done | bytes 655392 | tf_op jit(solution)/shard_map/all_to_all | solution.py:125
  27.6 0.7 multiply_add_fusion.2
  28.3 1.2 %fusion = f32[2,2,64,1280]{3,2,1,0:T(8,128)S(1)} fusion(f32[1,2,64,1280]{3,2,1,0:T(8,128)S(1)} %bitcast.45, f32[1,2,64,1280]{3,2,1,0:T(8,128)S(1)} %bitcast.44, f32[1,2,64,64]{3,2,1,0:T(8,128)S(1)} %get-tuple-element.13, f32[1,2,64,64]{3,2,1,0:T(8,128)S(1)} %get-tuple-element.14), kind=kOutput, calls=%fused_computation | convolution fusion | flops 252002304 | bytes 2686976 | tf_op jit(solution)/shard_map/sbkj,sbjl->sbkl/dot_general | solution.py:89
  29.6 0.1 fusion.67
  29.7 1.3 %fusion.4 = f32[2,2,64,1280]{3,2,1,0:T(8,128)S(1)} fusion(f32[2,2,64,1280]{3,2,1,0:T(8,128)S(1)} %fusion, f32[2,2,1280]{2,1,0:T(2,128)S(1)} %concatenate.18, f32[2,2,64]{2,1,0:T(2,128)S(1)} %pad_maximum_fusion.1, f32[1,2,64,64]{3,2,1,0:T(8,128)S(1)} %get-tuple-element.10, f32[1,2,64,64]{3,2,1,0:T(8,128)S(1)} %get-tuple-element.9), kind=kOutput, calls=%fused_computation.5 | convolution fusion | flops 252329984 | bytes 2708480 | tf_op jit(solution)/shard_map/sbkj,sbjl->sbkl/dot_general | solution.py:92
  31.0 0.1 fusion.66
  31.2 0.3 rev.7
  31.5 0.2 multiply_add_fusion
  31.6 2.1 %copy.12 = f32[2,128,1280]{2,0,1:T(2,128)} copy(f32[2,128,1280]{2,1,0:T(8,128)S(1)} %bitcast.42) | data formatting | bytes 2621440 | tf_op jit(solution)/shard_map/reshape | solution.py:132
  33.7 0.0 copy-start
  33.7 4.8 %all-to-all-start.1 = ((f32[2,128,1280]{2,0,1:T(2,128)}), f32[2,128,1280]{2,0,1:T(2,128)S(1)}, u32[]{:S(2)}, u32[]{:S(2)}) async-start(f32[2,128,1280]{2,0,1:T(2,128)} %copy.12), calls=%async_computation.1 | async-start | bytes 2621440 | tf_op jit(solution)/shard_map/all_to_all | solution.py:133
  38.5 0.0 copy-done
  38.5 0.1 fusion.65
  38.6 1.3 %collective-permute-start = (f32[8,5,8,3]{3,2,1,0:T(8,128)S(1)}, f32[8,5,8,3]{3,2,1,0:T(8,128)S(1)}, u32[]{:S(2)}, u32[]{:S(2)}) collective-permute-start(f32[8,5,8,3]{3,2,1,0:T(8,128)S(1)} %get-tuple-element.5), channel_id=1, source_target_pairs={{1,0},{3,2},{5,4},{7,6},{9,8},{11,10},{13,12},{15,14},{17,16},{19,... | collective-permute-start | bytes 11528 | tf_op jit(solution)/shard_map/ppermute | solution.py:19
  39.9 3.0 %collective-permute-start.1 = (f32[8,5,8,3]{3,2,1,0:T(8,128)S(1)}, f32[8,5,8,3]{3,2,1,0:T(8,128)S(1)}, u32[]{:S(2)}, u32[]{:S(2)}) collective-permute-start(f32[8,5,8,3]{3,2,1,0:T(8,128)S(1)} %get-tuple-element.6), channel_id=1, source_target_pairs={{0,1},{2,3},{4,5},{6,7},{8,9},{10,11},{12,13},{14,15},{16,17},{18,... | collective-permute-start | bytes 11528 | tf_op jit(solution)/shard_map/ppermute | solution.py:18
  43.0 0.0 collective-permute-done
  43.0 0.9 %collective-permute-done.1 = f32[8,5,8,3]{3,2,1,0:T(8,128)S(1)} collective-permute-done((f32[8,5,8,3]{3,2,1,0:T(8,128)S(1)}, f32[8,5,8,3]{3,2,1,0:T(8,128)S(1)}, u32[]{:S(2)}, u32[]{:S(2)}) %collective-permute-start.1) | collective-permute-done | bytes 3872 | tf_op jit(solution)/shard_map/ppermute | solution.py:18
  44.0 2.0 %fusion.12 = f32[8,5,8,512]{3,2,1,0:T(8,128)} fusion(f32[8,5,8,512]{3,2,1,0:T(8,128)S(1)} %copy-done, f32[8,5,8,3]{3,2,1,0:T(8,128)S(1)} %collective-permute-done.1, f32[8,5,8,515]{3,2,1,0:T(8,128)S(1)} %constant_dynamic-update-slice_fusion), kind=kLoop, calls=%fused_computation.17 | loop fusion | flops 1802240 | bytes 3280640 | tf_op jit(solution)/shard_map/div | solution.py:119
  46.0 23.0 %all-to-all-done.1 = f32[2,128,1280]{2,0,1:T(2,128)S(1)} async-done(((f32[2,128,1280]{2,0,1:T(2,128)}), f32[2,128,1280]{2,0,1:T(2,128)S(1)}, u32[]{:S(2)}, u32[]{:S(2)}) %all-to-all-start.1) | async-done | bytes 1310752 | tf_op jit(solution)/shard_map/all_to_all | solution.py:133
  69.0 1.0 %fusion.64 = (f32[1,8,16,1280]{3,0,1,2:T(1,128)S(1)}, f32[1,8,16,1280]{3,0,1,2:T(1,128)S(1)}) fusion(f32[2,8,16,1280]{3,0,1,2:T(2,128)S(1)} %bitcast.41), kind=kLoop, calls=%fused_computation.122 | loop fusion | bytes 2621440 | tf_op jit(solution)/shard_map/slice | solution.py:135
  70.0 0.2 copy.14
  70.3 1.0 %reshape_squeeze.7 = f32[8,5,8,512]{3,2,1,0:T(8,128)} reshape(f32[1,8,16,1280]{3,2,1,0:T(8,128)S(1)} %copy.14) | data formatting | bytes 1310720 | tf_op jit(solution)/shard_map/reshape;squeeze | solution.py:135
  71.3 0.2 copy.13
  71.5 1.0 %reshape_squeeze.6 = f32[8,5,8,512]{3,2,1,0:T(8,128)} reshape(f32[1,8,16,1280]{3,2,1,0:T(8,128)S(1)} %copy.13) | data formatting | bytes 1310720 | tf_op jit(solution)/shard_map/reshape;squeeze | solution.py:134
  (23 shorter events, 0.4 us)
Async XLA Ops:
  3.2 24.4 %all-to-all-start = ((f32[8,16,1280]{2,0,1:T(8,128)}), f32[8,16,1280]{2,0,1:T(8,128)S(1)}, u32[]{:S(2)}, u32[]{:S(2)}) async-start(f32[8,16,1280]{2,0,1:T(8,128)} %copy.11), calls=%async_computation | async-start | bytes 1310720 | tf_op jit(solution)/shard_map/all_to_all | solution.py:125
  33.7 4.8 %copy-start = (f32[8,5,8,512]{3,2,1,0:T(8,128)S(1)}, f32[8,5,8,512]{3,2,1,0:T(8,128)}, u32[]{:S(2)}) copy-start(f32[8,5,8,512]{3,2,1,0:T(8,128)} %param.1) | copy-start | bytes 1966084
  33.7 35.3 %all-to-all-start.1 = ((f32[2,128,1280]{2,0,1:T(2,128)}), f32[2,128,1280]{2,0,1:T(2,128)S(1)}, u32[]{:S(2)}, u32[]{:S(2)}) async-start(f32[2,128,1280]{2,0,1:T(2,128)} %copy.12), calls=%async_computation.1 | async-start | bytes 2621440 | tf_op jit(solution)/shard_map/all_to_all | solution.py:133
  38.6 4.4 %collective-permute-start = (f32[8,5,8,3]{3,2,1,0:T(8,128)S(1)}, f32[8,5,8,3]{3,2,1,0:T(8,128)S(1)}, u32[]{:S(2)}, u32[]{:S(2)}) collective-permute-start(f32[8,5,8,3]{3,2,1,0:T(8,128)S(1)} %get-tuple-element.5), channel_id=1, source_target_pairs={{1,0},{3,2},{5,4},{7,6},{9,8},{11,10},{13,12},{15,14},{17,16},{19,... | collective-permute-start | bytes 11528 | tf_op jit(solution)/shard_map/ppermute | solution.py:19
  39.9 4.1 %collective-permute-start.1 = (f32[8,5,8,3]{3,2,1,0:T(8,128)S(1)}, f32[8,5,8,3]{3,2,1,0:T(8,128)S(1)}, u32[]{:S(2)}, u32[]{:S(2)}) collective-permute-start(f32[8,5,8,3]{3,2,1,0:T(8,128)S(1)} %get-tuple-element.6), channel_id=1, source_target_pairs={{0,1},{2,3},{4,5},{6,7},{8,9},{10,11},{12,13},{14,15},{16,17},{18,... | collective-permute-start | bytes 11528 | tf_op jit(solution)/shard_map/ppermute | solution.py:18
where the time goes:
time: 72.9 us; the launch traced here: 72.5 us
  waiting for transfers between devices  39.2 us (54%)
  starting transfers between devices  16.3 us (22%)
  local copies, waits for them, and re-layouts  8.85 us (12%)
  other arithmetic  4.78 us (7%)
  matrix products  2.54 us (3%)
  between operations  0.86 us (1%)
    all_to_all x1, waiting for transfers between devices, body(): lax.all_to_all(solved, 'ax', split_axis=1, concat_axis=2, tiled=True)  23 us
    all_to_all x1, waiting for transfers between devices, body(): lines = lax.all_to_all(flat, 'ax', split_axis=1, concat_axis=0, tiled=True)  15.2 us
    all_to_all x1, starting transfers between devices, body(): lines = lax.all_to_all(flat, 'ax', split_axis=1, concat_axis=0, tiled=True)  7.22 us
    all_to_all x1, starting transfers between devices, body(): lax.all_to_all(solved, 'ax', split_axis=1, concat_axis=2, tiled=True)  4.77 us
    ppermute x1, starting transfers between devices, with_halo(): before = lax.ppermute(last, axis, up)  3.05 us
    all_to_all x2, local copies, waits for them, and re-layouts, body(): lines = lax.all_to_all(flat, 'ax', split_axis=1, concat_axis=0, tiled=True)  2.53 us
    reshape x1, local copies, waits for them, and re-layouts, body(): solved = solved.reshape(2, total, -1)  2.07 us
    div x1, other arithmetic, body(): (45.0 * (radial_cell(1) - radial_cell(-1)) - 9.0 * (radial_cell(2) - radi...  2.02 us
  transfers between devices with their start and end apart: 4, of which 3 were waited for; matrix products, arithmetic and copies ran while one was open for 6% of the time, Pallas kernels for 0%

commit v1 on v0

--- a/solution.py
+++ b/solution.py
@@ -122,7 +122,9 @@
         + (radial_cell(3) - radial_cell(-3))
     ) / 60.0
     flat = fields.reshape(rows_dev, width)
-    lines = lax.all_to_all(flat, "ax", split_axis=1, concat_axis=0, tiled=True)
+    lines = jnp.concatenate(
+        lax.all_to_all(jnp.stack(jnp.split(flat, lax.axis_size("ax"), axis=1)), "ax", 0, 0), axis=0
+    )
     total = lines.shape[0]
     padded = jnp.pad(lines, ((4, 4), (0, 0)))
     rhs = sources(padded, total)

time: 72.9 us -> 81.8 us (1.12)
  local copies, waits for them, and re-layouts: 8.85 us -> 17.7 us
    unnamed x5 -> x21, local copies, waits for them, and re-layouts: 0.07 us -> 10.8 us
    all_to_all x2 -> x0, local copies, waits for them, and re-layouts: 2.53 us -> none  [body(): lines = lax.all_to_all(flat, 'ax', split_axis=1, concat_axis=0, tiled=True)]
  transfers between devices with their start and end apart: 4 -> 4, of which waited for: 3 -> 3; matrix products, arithmetic and copies ran while one was open for 6% -> 5% of each run, Pallas kernels for 0% -> 0%
where the time goes in v1:
time: 81.8 us; the launch traced here: 81.4 us
  waiting for transfers between devices  39.2 us (48%)
  local copies, waits for them, and re-layouts  17.7 us (22%)
  starting transfers between devices  16.3 us (20%)
  other arithmetic  4.78 us (6%)
  matrix products  2.53 us (3%)
  between operations  0.87 us (1%)
    all_to_all x1, waiting for transfers between devices, body(): lax.all_to_all(solved, 'ax', split_axis=1, concat_axis=2, tiled=True)  23 us
    all_to_all x1, waiting for transfers between devices, body(): lax.all_to_all(jnp.stack(jnp.split(flat, lax.axis_size('ax'), axis=1)), '...  15.2 us
    unnamed x21, local copies, waits for them, and re-layouts  10.8 us
    all_to_all x1, starting transfers between devices, body(): lax.all_to_all(jnp.stack(jnp.split(flat, lax.axis_size('ax'), axis=1)), '...  7.22 us
    all_to_all x1, starting transfers between devices, body(): lax.all_to_all(solved, 'ax', split_axis=1, concat_axis=2, tiled=True)  4.78 us
    ppermute x1, starting transfers between devices, with_halo(): before = lax.ppermute(last, axis, up)  3.05 us
    reshape x1, local copies, waits for them, and re-layouts, body(): solved = solved.reshape(2, total, -1)  2.07 us
    div x1, other arithmetic, body(): (45.0 * (radial_cell(1) - radial_cell(-1)) - 9.0 * (radial_cell(2) - radi...  2.02 us
  transfers between devices with their start and end apart: 4, of which 3 were waited for; matrix products, arithmetic and copies ran while one was open for 5% of the time, Pallas kernels for 0%

profile of v1, /device:TPU:8, one launch (start us, length us, event | category | flops | bytes accessed | tf_op | source)
XLA Modules:
  0.0 81.4 jit_solution(4989583152934408210)
XLA Ops:
  0.6 1.5 %copy.11 = f32[1,8,40,512]{3,1,2,0:T(8,128)S(1)} copy(f32[1,8,40,512]{3,2,1,0:T(8,128)} %bitcast.104) | data formatting | bytes 1310720
  2.1 0.6 fusion.40
  2.7 0.6 fusion.39
  3.3 0.6 fusion.38
  4.0 0.6 fusion.37
  4.6 0.6 fusion.36
  5.2 0.6 fusion.35
  5.8 0.6 fusion.34
  6.4 0.6 fusion.33
  7.1 0.6 fusion.32
  7.7 0.6 fusion.31
  8.3 0.6 fusion.30
  8.9 0.6 fusion.29
  9.6 0.6 fusion.28
  10.2 0.6 fusion.27
  10.8 0.6 fusion.26
  11.4 0.6 fusion.25
  12.0 7.2 %all-to-all-start = ((f32[16,8,1280]{2,1,0:T(8,128)}), f32[16,8,1280]{2,1,0:T(8,128)S(1)}, u32[]{:S(2)}, u32[]{:S(2)}) async-start(f32[16,8,1280]{2,1,0:T(8,128)} %fusion.25), calls=%async_computation | async-start | bytes 1310720 | tf_op jit(solution)/shard_map/all_to_all | solution.py:126
  19.4 0.2 reduce_window_sum.36
  19.7 0.2 reduce_window_sum.29
  19.9 0.2 reduce_window_sum.28
  20.1 0.2 reduce_window_sum.27
  20.4 0.2 slice_reduce_fusion
  20.6 0.1 fusion.55
  20.7 0.1 fusion.65
  20.8 0.2 fusion.64
  21.1 0.1 divide_select_fusion.1
  21.3 15.2 %all-to-all-done = f32[16,8,1280]{2,1,0:T(8,128)S(1)} async-done(((f32[16,8,1280]{2,1,0:T(8,128)}), f32[16,8,1280]{2,1,0:T(8,128)S(1)}, u32[]{:S(2)}, u32[]{:S(2)}) %all-to-all-start) | async-done | bytes 655392 | tf_op jit(solution)/shard_map/all_to_all | solution.py:126
  36.5 0.7 multiply_add_fusion.2
  37.1 1.2 %fusion = f32[2,2,64,1280]{3,2,1,0:T(8,128)S(1)} fusion(f32[1,2,64,1280]{3,2,1,0:T(8,128)S(1)} %bitcast.109, f32[1,2,64,1280]{3,2,1,0:T(8,128)S(1)} %bitcast.108, f32[1,2,64,64]{3,2,1,0:T(8,128)S(1)} %get-tuple-element.13, f32[1,2,64,64]{3,2,1,0:T(8,128)S(1)} %get-tuple-element.14), kind=kOutput, calls=%fused_computation | convolution fusion | flops 252002304 | bytes 2686976 | tf_op jit(solution)/shard_map/sbkj,sbjl->sbkl/dot_general | solution.py:89
  38.4 0.1 fusion.83
  38.5 1.3 %fusion.4 = f32[2,2,64,1280]{3,2,1,0:T(8,128)S(1)} fusion(f32[2,2,64,1280]{3,2,1,0:T(8,128)S(1)} %fusion, f32[2,2,1280]{2,1,0:T(2,128)S(1)} %concatenate.18, f32[2,2,64]{2,1,0:T(2,128)S(1)} %pad_maximum_fusion.1, f32[1,2,64,64]{3,2,1,0:T(8,128)S(1)} %get-tuple-element.10, f32[1,2,64,64]{3,2,1,0:T(8,128)S(1)} %get-tuple-element.9), kind=kOutput, calls=%fused_computation.5 | convolution fusion | flops 252329984 | bytes 2708480 | tf_op jit(solution)/shard_map/sbkj,sbjl->sbkl/dot_general | solution.py:92
  39.9 0.1 fusion.82
  40.0 0.3 rev.7
  40.3 0.2 multiply_add_fusion
  40.5 2.1 %copy.6 = f32[2,128,1280]{2,0,1:T(2,128)} copy(f32[2,128,1280]{2,1,0:T(8,128)S(1)} %bitcast.106) | data formatting | bytes 2621440 | tf_op jit(solution)/shard_map/reshape | solution.py:134
  42.6 4.8 %all-to-all-start.1 = ((f32[2,128,1280]{2,0,1:T(2,128)}), f32[2,128,1280]{2,0,1:T(2,128)S(1)}, u32[]{:S(2)}, u32[]{:S(2)}) async-start(f32[2,128,1280]{2,0,1:T(2,128)} %copy.6), calls=%async_computation.1 | async-start | bytes 2621440 | tf_op jit(solution)/shard_map/all_to_all | solution.py:135
  47.4 0.1 fusion.81
  47.5 1.3 %collective-permute-start = (f32[8,5,8,3]{3,2,1,0:T(8,128)S(1)}, f32[8,5,8,3]{3,2,1,0:T(8,128)S(1)}, u32[]{:S(2)}, u32[]{:S(2)}) collective-permute-start(f32[8,5,8,3]{3,2,1,0:T(8,128)S(1)} %get-tuple-element.5), channel_id=1, source_target_pairs={{1,0},{3,2},{5,4},{7,6},{9,8},{11,10},{13,12},{15,14},{17,16},{19,... | collective-permute-start | bytes 11528 | tf_op jit(solution)/shard_map/ppermute | solution.py:19
  48.8 3.0 %collective-permute-start.1 = (f32[8,5,8,3]{3,2,1,0:T(8,128)S(1)}, f32[8,5,8,3]{3,2,1,0:T(8,128)S(1)}, u32[]{:S(2)}, u32[]{:S(2)}) collective-permute-start(f32[8,5,8,3]{3,2,1,0:T(8,128)S(1)} %get-tuple-element.6), channel_id=1, source_target_pairs={{0,1},{2,3},{4,5},{6,7},{8,9},{10,11},{12,13},{14,15},{16,17},{18,... | collective-permute-start | bytes 11528 | tf_op jit(solution)/shard_map/ppermute | solution.py:18
  51.9 0.9 %collective-permute-done.1 = f32[8,5,8,3]{3,2,1,0:T(8,128)S(1)} collective-permute-done((f32[8,5,8,3]{3,2,1,0:T(8,128)S(1)}, f32[8,5,8,3]{3,2,1,0:T(8,128)S(1)}, u32[]{:S(2)}, u32[]{:S(2)}) %collective-permute-start.1) | collective-permute-done | bytes 3872 | tf_op jit(solution)/shard_map/ppermute | solution.py:18
  52.8 2.0 %fusion.12 = f32[8,5,8,512]{3,2,1,0:T(8,128)} fusion(f32[8,5,8,512]{3,2,1,0:T(8,128)S(1)} %copy-done, f32[8,5,8,3]{3,2,1,0:T(8,128)S(1)} %collective-permute-done.1, f32[8,5,8,515]{3,2,1,0:T(8,128)S(1)} %constant_dynamic-update-slice_fusion), kind=kLoop, calls=%fused_computation.17 | loop fusion | flops 1802240 | bytes 3280640 | tf_op jit(solution)/shard_map/div | solution.py:119
  54.9 23.0 %all-to-all-done.1 = f32[2,128,1280]{2,0,1:T(2,128)S(1)} async-done(((f32[2,128,1280]{2,0,1:T(2,128)}), f32[2,128,1280]{2,0,1:T(2,128)S(1)}, u32[]{:S(2)}, u32[]{:S(2)}) %all-to-all-start.1) | async-done | bytes 1310752 | tf_op jit(solution)/shard_map/all_to_all | solution.py:135
  77.9 1.0 %fusion.80 = (f32[1,8,16,1280]{3,0,1,2:T(1,128)S(1)}, f32[1,8,16,1280]{3,0,1,2:T(1,128)S(1)}) fusion(f32[2,8,16,1280]{3,0,1,2:T(2,128)S(1)} %bitcast.105), kind=kLoop, calls=%fused_computation.154 | loop fusion | bytes 2621440 | tf_op jit(solution)/shard_map/slice | solution.py:137
  78.9 0.2 copy.8
  79.1 1.0 %reshape_squeeze.7 = f32[8,5,8,512]{3,2,1,0:T(8,128)} reshape(f32[1,8,16,1280]{3,2,1,0:T(8,128)S(1)} %copy.8) | data formatting | bytes 1310720 | tf_op jit(solution)/shard_map/reshape;squeeze | solution.py:137
  80.2 0.2 copy.7
  80.4 1.0 %reshape_squeeze.6 = f32[8,5,8,512]{3,2,1,0:T(8,128)} reshape(f32[1,8,16,1280]{3,2,1,0:T(8,128)S(1)} %copy.7) | data formatting | bytes 1310720 | tf_op jit(solution)/shard_map/reshape;squeeze | solution.py:136
  (26 shorter events, 0.4 us)
Async XLA Ops:
  12.0 24.4 %all-to-all-start = ((f32[16,8,1280]{2,1,0:T(8,128)}), f32[16,8,1280]{2,1,0:T(8,128)S(1)}, u32[]{:S(2)}, u32[]{:S(2)}) async-start(f32[16,8,1280]{2,1,0:T(8,128)} %fusion.25), calls=%async_computation | async-start | bytes 1310720 | tf_op jit(solution)/shard_map/all_to_all | solution.py:126
  42.6 4.8 %copy-start = (f32[8,5,8,512]{3,2,1,0:T(8,128)S(1)}, f32[8,5,8,512]{3,2,1,0:T(8,128)}, u32[]{:S(2)}) copy-start(f32[8,5,8,512]{3,2,1,0:T(8,128)} %param.1) | copy-start | bytes 1966084
  42.6 35.3 %all-to-all-start.1 = ((f32[2,128,1280]{2,0,1:T(2,128)}), f32[2,128,1280]{2,0,1:T(2,128)S(1)}, u32[]{:S(2)}, u32[]{:S(2)}) async-start(f32[2,128,1280]{2,0,1:T(2,128)} %copy.6), calls=%async_computation.1 | async-start | bytes 2621440 | tf_op jit(solution)/shard_map/all_to_all | solution.py:135
  47.5 4.4 %collective-permute-start = (f32[8,5,8,3]{3,2,1,0:T(8,128)S(1)}, f32[8,5,8,3]{3,2,1,0:T(8,128)S(1)}, u32[]{:S(2)}, u32[]{:S(2)}) collective-permute-start(f32[8,5,8,3]{3,2,1,0:T(8,128)S(1)} %get-tuple-element.5), channel_id=1, source_target_pairs={{1,0},{3,2},{5,4},{7,6},{9,8},{11,10},{13,12},{15,14},{17,16},{19,... | collective-permute-start | bytes 11528 | tf_op jit(solution)/shard_map/ppermute | solution.py:19
  48.8 4.1 %collective-permute-start.1 = (f32[8,5,8,3]{3,2,1,0:T(8,128)S(1)}, f32[8,5,8,3]{3,2,1,0:T(8,128)S(1)}, u32[]{:S(2)}, u32[]{:S(2)}) collective-permute-start(f32[8,5,8,3]{3,2,1,0:T(8,128)S(1)} %get-tuple-element.6), channel_id=1, source_target_pairs={{0,1},{2,3},{4,5},{6,7},{8,9},{10,11},{12,13},{14,15},{16,17},{18,... | collective-permute-start | bytes 11528 | tf_op jit(solution)/shard_map/ppermute | solution.py:18
